TPU v7x, 32 devices: a whole 2x2x4 slice. The times are simulated.
32 devices in a mesh: grp: 4 (over y, x), dev: 8 (over z, core).
Axes of the slice: x: 2, y: 2, z: 4, core: 2. Of those that a mesh axis runs over, the one named last changes fastest.
Arguments:
- image_tokens: bfloat16 [128, 197, 768], P(('grp', 'dev')), may hold values from -64 to 64
- text_tokens: bfloat16 [128, 30, 768], P(('grp', 'dev')), may hold values from -64 to 64
- negatives: int32 [128, 2], P(('grp', 'dev')), may hold values from 0 to 31, as said below
- query_weight: bfloat16 [768, 768], replicated, may hold values from -0.21875 to 0.21875
- kv_weight: bfloat16 [768, 1536], replicated, may hold values from -0.21875 to 0.21875
- match_head: float32 [768], replicated, may hold values from -6 to 6
- cotangent: bfloat16 [128, 3], P(('grp', 'dev')), may hold values from -6 to 6
Outputs:
- logits: float32 [128, 3], P(('grp', 'dev'))
- grad_query_weight: float32 [768, 768], P(('grp', 'dev'))
- grad_kv_weight: float32 [768, 1536], P(('grp', 'dev'))
Inputs may be any that keep to these rules, and one draw needn't show every extreme that they name: At most 2 of the 8 negatives of one device lie on any one device of its group, and in every group some device holds exactly 2 negatives of every device of the group.
All inputs are finite; a program needn't handle non-finite values.
Results may differ from a plain program's by a relative error of at most 0.0085.
The roundings to bfloat16 on the way count: a program that leaves them out, or rounds other values in their place, can miss the bound.
Values may be sent and summed in bfloat16 or wider, within the bound.
A program may use at most 128 MiB of HBM per device.

v0:
```python
import jax
import jax.numpy as jnp
from jax import lax
from jax.sharding import PartitionSpec as P

HEADS = 12


def project(tokens, weight):
    count, length, model = tokens.shape
    flat = jnp.dot(tokens.reshape(-1, model), weight, preferred_element_type=jnp.float32)
    return flat.astype(jnp.bfloat16).reshape(count, length, weight.shape[1])


def outer_rows(pictures, grads):
    model = pictures.shape[-1]
    return lax.dot_general(
        pictures.reshape(-1, model),
        grads.reshape(-1, grads.shape[-1]),
        (((0,), (0,)), ((), ())),
        preferred_element_type=jnp.float32,
    )


def attend(queries, keys_values, tangent, match_head):
    count = queries.shape[0]
    text_len = queries.shape[1]
    image_len = keys_values.shape[1]
    model = queries.shape[2]
    head_size = model // HEADS
    factor = head_size ** (-0.5)
    query_heads = queries.reshape(count, text_len, HEADS, head_size)
    key_heads = keys_values[..., :model].reshape(count, image_len, HEADS, head_size)
    value_heads = keys_values[..., model:].reshape(count, image_len, HEADS, head_size)
    scores = (
        jnp.einsum("bqhd,bkhd->bhqk", query_heads, key_heads, preferred_element_type=jnp.float32)
        * factor
    )
    probs = jax.nn.softmax(scores, axis=-1)
    probs_low = probs.astype(jnp.bfloat16)
    context = jnp.einsum(
        "bhqk,bkhd->bqhd", probs_low, value_heads, preferred_element_type=jnp.float32
    )
    pooled = jnp.mean(context, axis=1).reshape(count, model)
    logits = jnp.sum(pooled * match_head[None, :], axis=-1)
    direction = (tangent / text_len)[:, None] * match_head[None, :]
    dir_heads = direction.reshape(count, HEADS, head_size)
    d_probs = jnp.einsum(
        "bkhd,bhd->bhk", value_heads.astype(jnp.float32), dir_heads, precision=lax.Precision.HIGHEST
    )
    d_scores = probs * (
        d_probs[:, :, None, :] - jnp.sum(probs * d_probs[:, :, None, :], axis=-1, keepdims=True)
    )
    d_low = d_scores.astype(jnp.bfloat16)
    d_keys = (
        jnp.einsum("bhqk,bqhd->bkhd", d_low, query_heads, preferred_element_type=jnp.float32)
        * factor
    )
    d_queries = (
        jnp.einsum("bhqk,bkhd->bqhd", d_low, key_heads, preferred_element_type=jnp.float32) * factor
    )
    weight_sum = jnp.sum(probs_low.astype(jnp.float32), axis=2)
    d_values = jnp.transpose(weight_sum[..., None] * dir_heads[:, :, None, :], (0, 2, 1, 3))
    kv_grad = jnp.concatenate(
        [d_keys.reshape(count, image_len, model), d_values.reshape(count, image_len, model)],
        axis=-1,
    )
    return (logits, kv_grad, d_queries.reshape(count, text_len, model))


def routing(negatives, pair_count, capacity):
    wanted = negatives.reshape(-1)
    owner = wanted // pair_count
    local_image = wanted % pair_count
    order = jnp.arange(wanted.shape[0], dtype=jnp.int32)
    earlier = (owner[:, None] == owner[None, :]) & (order[None, :] < order[:, None])
    rank = jnp.sum(earlier.astype(jnp.int32), axis=1)
    return (local_image, owner * capacity + rank)


def slot_table(local_image, place, slot_count):
    order = jnp.arange(place.shape[0], dtype=jnp.int32)
    matches = jnp.arange(slot_count, dtype=jnp.int32)[:, None] == place[None, :]
    table = jnp.sum(jnp.where(matches, local_image[None, :], 0), axis=1)
    source = jnp.sum(jnp.where(matches, order[None, :], 0), axis=1)
    used = jnp.any(matches, axis=1)
    return (table, source, used)


def local(image_tokens, text_tokens, negatives, query_weight, kv_weight, match_head, cotangent):
    pair_count = text_tokens.shape[0]
    text_len = text_tokens.shape[1]
    image_len = image_tokens.shape[1]
    model = text_tokens.shape[2]
    devices = lax.axis_size("dev")
    capacity = max(2, (2 * pair_count + devices - 1) // devices)
    slot_count = devices * capacity
    tangent = cotangent.astype(jnp.float32)
    queries = project(text_tokens, query_weight)
    local_image, place = routing(negatives, pair_count, capacity)
    table, source, used = slot_table(local_image, place, slot_count)
    asked = lax.all_to_all(
        table.reshape(devices, capacity), "dev", split_axis=0, concat_axis=0, tiled=True
    )
    outgoing = image_tokens[asked.reshape(-1)].reshape(devices, capacity, image_len, model)
    arrived = lax.all_to_all(outgoing, "dev", split_axis=0, concat_axis=0, tiled=True)
    fetched = arrived.reshape(slot_count, image_len, model)[place].reshape(
        pair_count, 2, image_len, model
    )
    pictures = jnp.concatenate([image_tokens, fetched[:, 0], fetched[:, 1]], axis=0)
    keys_values = project(pictures, kv_weight)
    all_queries = jnp.concatenate([queries, queries, queries], axis=0)
    all_tangent = jnp.concatenate([tangent[:, 0], tangent[:, 1], tangent[:, 2]], axis=0)
    flat_logits, kv_grad, part_grad = attend(all_queries, keys_values, all_tangent, match_head)
    grad_kv = outer_rows(pictures, kv_grad.astype(jnp.bfloat16))
    query_grad = jnp.sum(part_grad.reshape(3, pair_count, text_len, model), axis=0)
    logits = jnp.transpose(flat_logits.reshape(3, pair_count), (1, 0))
    grad_query = outer_rows(text_tokens, query_grad.astype(jnp.bfloat16))
    grad_query_weight, grad_kv_weight = (
        lax.psum_scatter(grad_query, ("grp", "dev"), scatter_dimension=0, tiled=True),
        lax.psum_scatter(grad_kv, ("grp", "dev"), scatter_dimension=0, tiled=True),
    )
    return (logits, grad_query_weight, grad_kv_weight)


def solution(mesh):
    placed = (
        P(("grp", "dev"), None, None),
        P(("grp", "dev"), None, None),
        P(("grp", "dev"), None),
        P(),
        P(),
        P(),
        P(("grp", "dev"), None),
    )
    return jax.shard_map(
        local,
        mesh=mesh,
        in_specs=placed,
        out_specs=(P(("grp", "dev"), None), P(("grp", "dev"), None), P(("grp", "dev"), None)),
        check_vma=False,
    )
```

profile of v0, /device:TPU:0, one launch (start us, length us, event | category | flops | bytes accessed | tf_op | source)
XLA Modules:
  0.0 482.4 jit_solution(5439957624436056736)
XLA Ops:
  7.2 0.9 copy.61
  8.1 0.1 reshape.314
  8.2 0.2 convert_reduce_fusion.1
  8.4 0.5 copy-done.14
  8.9 0.1 select_reduce_fusion
  9.0 0.1 all_to_all.9
  9.1 11.7 %all_to_all.14 = s32[8,1,2]{2,1,0:T(1,128)S(1)} all-to-all(s32[8,1,2]{2,1,0:T(1,128)S(1)} %bitcast.69), channel_id=1, replica_groups=mesh['grp'=4,'dev'=8] {'dev'}, dimensions={0} | all-to-all | bytes 128 | tf_op jit(solution)/shard_map/all_to_all | solution.py:102
  20.7 0.5 broadcast.277
  21.2 0.7 reduce.11
  21.9 0.1 reshape.315
  22.0 15.0 %gather_fusion = bf16[16,197,768]{2,0,1:T(8,128)(2,1)} fusion(bf16[4,197,768]{2,0,1:T(4,128)(2,1)} %param.7, s32[1024]{0:T(1024)S(1)} %pad_clamp_fusion.1), kind=kCustom, calls=%fused_computation | custom fusion | bytes 9683008 | tf_op jit(solution)/shard_map/gather | solution.py:105
  37.0 10.7 %reshape.316 = bf16[8,2,197,768]{3,1,0,2:T(2,128)(2,1)} reshape(bf16[16,197,768]{2,0,1:T(8,128)(2,1)} %gather_fusion) | data formatting | bytes 9682944 | tf_op jit(solution)/shard_map/reshape | solution.py:105
  47.8 7.9 %copy.63 = bf16[8,2,197,768]{3,1,2,0:T(2,128)(2,1)} copy(bf16[8,2,197,768]{3,1,0,2:T(2,128)(2,1)} %reshape.316) | data formatting | bytes 9682944 | tf_op jit(solution)/shard_map/reshape | solution.py:105
  55.6 4.7 all-to-all-start.1
  60.4 0.6 reshape.318
  61.0 2.5 copy.68
  63.6 1.6 copy.70
  65.2 1.7 reshape.323
  66.9 1.9 convolution_convert_fusion.1
  68.8 1.2 concatenate.27
  70.0 0.2 slice_reduce_fusion.2
  70.2 0.1 maximum_multiply_fusion
  70.3 0.7 fusion.18
  71.0 0.1 multiply_bitcast_fusion.1
  71.1 0.9 copy_dynamic-update-slice_fusion.1
  71.9 0.9 copy_dynamic-update-slice_fusion
  72.8 0.9 copy_dynamic-update-slice_fusion.2
  73.7 94.6 %all-to-all-done.1 = bf16[8,2,197,768]{3,1,2,0:T(2,128)(2,1)} async-done(((bf16[8,2,197,768]{3,1,2,0:T(2,128)(2,1)}), bf16[8,2,197,768]{3,1,2,0:T(2,128)(2,1)}, u32[]{:S(2)}, u32[]{:S(2)}) %all-to-all-start.1) | async-done | bytes 4841504 | tf_op jit(solution)/shard_map/all_to_all | solution.py:106
  168.3 5.2 %copy.64 = bf16[8,2,197,768]{3,2,1,0:T(8,128)(2,1)} copy(bf16[8,2,197,768]{3,1,2,0:T(2,128)(2,1)} %all-to-all-done.1) | data formatting | bytes 9682944 | tf_op jit(solution)/shard_map/all_to_all | solution.py:106
  173.5 4.6 gather_fusion.1
  178.1 1.9 slice_bitcast_fusion.1
  180.0 1.0 copy-done.5
  181.0 0.4 copy-done.7
  181.4 2.5 pad_maximum_fusion
  183.9 4.2 reshape.320
  188.2 9.9 %convolution_convert_fusion = bf16[2364,1536]{1,0:T(8,128)(2,1)} fusion(bf16[2364,768]{1,0:T(8,128)(2,1)} %reshape.320, bf16[768,1536]{1,0:T(8,128)(2,1)S(1)} %copy-done), kind=kOutput, calls=%fused_computation.3 | convolution fusion | flops 5581006848 | bytes 13252608 | tf_op jit(solution)/shard_map/dot_general | solution.py:11
  198.1 9.8 %reshape.321 = bf16[12,197,1536]{2,1,0:T(8,128)(2,1)} reshape(bf16[2364,1536]{1,0:T(8,128)(2,1)} %convolution_convert_fusion) | data formatting | bytes 14524416 | tf_op jit(solution)/shard_map/reshape | solution.py:12
  207.9 6.7 %fusion.22 = (bf16[12,197,768]{2,1,0:T(8,128)(2,1)}, bf16[12,197,768]{2,1,0:T(8,128)(2,1)}) fusion(bf16[12,197,1536]{2,1,0:T(8,128)(2,1)} %reshape.321), kind=kLoop, calls=%fused_computation.67 | loop fusion | bytes 14524416 | tf_op jit(solution)/shard_map/slice | solution.py:33
  214.5 6.3 %copy.74 = bf16[12,197,768]{1,2,0:T(8,128)(2,1)} copy(bf16[12,197,768]{2,1,0:T(8,128)(2,1)} %get-tuple-element.20) | data formatting | bytes 7262208 | tf_op jit(solution)/shard_map/slice | solution.py:33
  220.8 6.3 %copy.69 = bf16[12,197,768]{1,2,0:T(8,128)(2,1)} copy(bf16[12,197,768]{2,1,0:T(8,128)(2,1)} %get-tuple-element.21) | data formatting | bytes 7262208 | tf_op jit(solution)/shard_map/slice | solution.py:34
  227.1 4.3 fusion.14
  231.4 6.3 %fusion.23 = (f32[12,12,30]{2,1,0:T(8,128)S(1)}, f32[12,12,30,197]{3,2,1,0:T(8,128)}) fusion(bf16[12,30,12,64]{3,1,2,0:T(8,128)(2,1)} %copy_dynamic-update-slice_fusion.2, bf16[12,197,12,64]{1,3,2,0:T(8,128)(2,1)} %bitcast.60), kind=kOutput, calls=%fused_computation.68 | convolution fusion | flops 111486432 | bytes 7605504 | tf_op jit(solution)/shard_map/sub | solution.py:39
  237.7 3.7 convert_reduce_fusion
  241.5 15.0 %multiply_bitcast_fusion = f32[12,30,12,64]{3,1,2,0:T(8,128)S(1)} fusion(bf16[12,197,12,64]{1,3,2,0:T(8,128)(2,1)} %bitcast.61, f32[12,12,30]{2,1,0:T(8,128)S(1)} %get-tuple-element.16, f32[12,12,197]{2,1,0:T(8,128)S(1)} %bitcast.66, f32[12,12,30,197]{3,2,1,0:T(8,128)S(1)} %copy-done.2, f32[12,12,30]{2,1,0:T(8,128)S(1)} %get-tuple-element.26), kind=kOutput, calls=%fused_computation.18 | convolution fusion | flops 112613760 | bytes 8289216 | tf_op jit(solution)/shard_map/bhqk,bkhd->bqhd/dot_general | solution.py:60
  256.5 2.9 copy.75
  259.5 2.5 reshape_reshape.3
  261.9 0.4 reduce_sum.81
  262.3 0.5 convolution_bitcast_fusion
  262.8 2.0 copy.84
  264.8 0.1 broadcast_multiply_fusion
  264.9 7.0 %multiply_convert_fusion = bf16[12,12,64,197]{3,2,1,0:T(8,128)(2,1)} fusion(bf16[12,30,12,64]{3,1,2,0:T(8,128)(2,1)} %copy_dynamic-update-slice_fusion.2, f32[12,12,30]{2,1,0:T(8,128)S(1)} %get-tuple-element.16, f32[12,12,197]{2,1,0:T(8,128)S(1)} %bitcast.67, f32[12,12,30,197]{3,2,1,0:T(8,128)} %get-tuple-element.27, f32[12,12,30]{2,1,0:T(8,128)S(1)} %get-tuple-element.26), kind=kOutput, calls=%fused_computation.4 | convolution fusion | flops 115968384 | bytes 7736256 | tf_op jit(solution)/shard_map/bhqk,bqhd->bkhd/dot_general | solution.py:56
  271.9 6.4 %copy.79 = bf16[12,197,768]{2,1,0:T(8,128)(2,1)} copy(bf16[12,197,768]{1,2,0:T(8,128)(2,1)} %bitcast.64) | data formatting | bytes 7262208 | tf_op jit(solution)/shard_map/reshape | solution.py:65
  278.3 4.4 mul.128
  282.7 9.0 %copy.78 = f32[12,197,768]{2,1,0:T(8,128)} copy(f32[12,197,768]{1,2,0:T(8,128)} %bitcast.57) | data formatting | bytes 14524416 | tf_op jit(solution)/shard_map/mul | solution.py:63
  291.8 4.0 multiply_convert_fusion.1
  295.8 0.3 copy-done.8
  296.0 1.2 copy-done.9
  297.2 8.6 %fusion.6 = f32[768,1536]{1,0:T(8,128)} fusion(bf16[12,197,768]{2,1,0:T(8,128)(2,1)S(1)} %multiply_convert_fusion.1, bf16[12,197,768]{2,1,0:T(8,128)(2,1)S(1)} %copy-done.9, bf16[4,197,768]{2,1,0:T(8,128)(2,1)S(1)} %copy-done.8, bf16[4,197,768]{2,1,0:T(8,128)(2,1)S(1)} %copy-done.6, bf16[4,197,768]{2,1,0:T(8,128)(2,1)S(1)} %copy-done.4), kind=kOutput, calls=%fused_computation.16 | convolution fusion | flops 5595531264 | bytes 15611904 | tf_op jit(solution)/shard_map/dot_general | solution.py:17
  305.9 5.3 %convolution_reduce_fusion = f32[12,12,64]{2,1,0:T(8,128)S(1)} fusion(bf16[12,197,12,64]{1,3,2,0:T(8,128)(2,1)} %bitcast.59, f32[12,12,30,197]{3,2,1,0:T(8,128)} %get-tuple-element.27, f32[12,12,30]{2,1,0:T(8,128)S(1)} %get-tuple-element.26), kind=kOutput, calls=%fused_computation.22 | convolution fusion | flops 110902464 | bytes 7089408 | tf_op jit(solution)/shard_map/bhqk,bkhd->bqhd/dot_general | solution.py:41
  311.2 0.2 multiply_reduce_fusion.2
  311.4 0.1 reshape.325
  311.5 0.7 copy.80
  312.1 50.2 %reduce-scatter.7.cloned.1.call-done = f32[24,768]{1,0:T(8,128)} async-done(((f32[768,768]{1,0:T(8,128)}), f32[24,768]{1,0:T(8,128)}) %reduce-scatter.7.cloned.1.call-update) | async-done | bytes 73744
  362.4 113.0 %reduce-scatter.5.cloned.1.call-done = f32[24,1536]{1,0:T(8,128)} async-done(((f32[768,1536]{1,0:T(8,128)}), f32[24,1536]{1,0:T(8,128)}) %reduce-scatter.5.cloned.1.call-update) | async-done | bytes 147472 | tf_op jit(solution)/shard_map/reduce_scatter | solution.py:121
  (38 shorter events, 0.3 us)
Async XLA Ops:
  7.2 181.0 %copy-start = (bf16[768,1536]{1,0:T(8,128)(2,1)S(1)}, bf16[768,1536]{1,0:T(8,128)(2,1)}, u32[]{:S(2)}) copy-start(bf16[768,1536]{1,0:T(8,128)(2,1)} %param.11) | copy-start | bytes 7077892
  8.4 0.5 copy-start.14
  55.6 7.9 %copy-start.13 = (bf16[4,3]{1,0:T(4,128)(2,1)S(1)}, bf16[4,3]{1,0:T(4,128)(2,1)}, u32[]{:S(2)}) copy-start(bf16[4,3]{1,0:T(4,128)(2,1)} %param.13) | copy-start | bytes 76
  55.6 7.9 %copy-start.12 = (f32[768]{0:T(1024)S(1)}, f32[768]{0:T(1024)}, u32[]{:S(2)}) copy-start(f32[768]{0:T(1024)} %param.12) | copy-start | bytes 9220
  55.6 11.2 %copy-start.10 = (bf16[768,768]{1,0:T(8,128)(2,1)S(1)}, bf16[768,768]{1,0:T(8,128)(2,1)}, u32[]{:S(2)}) copy-start(bf16[768,768]{1,0:T(8,128)(2,1)} %param.10) | copy-start | bytes 3538948
  55.6 112.6 %all-to-all-start.1 = ((bf16[8,2,197,768]{3,1,2,0:T(2,128)(2,1)}), bf16[8,2,197,768]{3,1,2,0:T(2,128)(2,1)}, u32[]{:S(2)}, u32[]{:S(2)}) async-start(bf16[8,2,197,768]{3,1,2,0:T(2,128)(2,1)} %copy.63), calls=%async_computation.1 | async-start | bytes 9682944 | tf_op jit(solution)/shard_map/all_to_all | solution.py:106
  60.4 302.0 %reduce-scatter.7.cloned.1.call-start = ((), (), s32[]{:S(2)}) async-start(), calls=%async_computation.5 | async-start | bytes 2433024
  178.0 3.3 copy-start.3
  180.0 1.1 copy-start.5
  180.0 1.4 copy-start.7
  237.7 3.8 copy-start.2
  259.4 2.8 copy-start.11
  264.8 210.6 %reduce-scatter.5.cloned.1.call-start = ((), (), s32[]{:S(2)}) async-start(), calls=%async_computation.4 | async-start | bytes 4866048 | tf_op jit(solution)/shard_map/reduce_scatter | solution.py:121
  291.8 4.0 copy-start.4
  291.8 4.0 copy-start.6
  291.8 4.3 copy-start.8
  291.8 5.5 %copy-start.9 = (bf16[12,197,768]{2,1,0:T(8,128)(2,1)S(1)}, bf16[12,197,768]{2,1,0:T(8,128)(2,1)}, u32[]{:S(2)}) copy-start(bf16[12,197,768]{2,1,0:T(8,128)(2,1)} %copy.79) | copy-start | bytes 10893316
  305.8 169.5 %copy-start.1 = (bf16[768,1536]{1,0:T(8,128)(2,1)S(1)}, bf16[768,1536]{1,0:T(8,128)(2,1)}, u32[]{:S(2)}) copy-start(bf16[768,1536]{1,0:T(8,128)(2,1)} %param.11) | copy-start | bytes 7077892
Sparse Core Ops, SparseCore 0:
  264.9 97.4 reduce-scatter.6
  369.3 106.0 reduce-scatter.4
where the time goes:
time: 485 us; the launch traced here: 482 us
  waiting for transfers between devices  258 us (53%)
  local copies, waits for them, and re-layouts  122 us (25%)
  matrix products  59 us (12%)
  between operations  14.4 us (3%)
  other arithmetic  12.6 us (3%)
  blocking collectives  11.7 us (2%)
    reduce_scatter x1, waiting for transfers between devices, local(): lax.psum_scatter(grad_kv, ('grp', 'dev'), scatter_dimension=0, tiled=True)  113 us
    all_to_all x1, waiting for transfers between devices, local(): lax.all_to_all(outgoing, 'dev', split_axis=0, concat_axis=0, tiled=True)  94.6 us
    unnamed x3, waiting for transfers between devices  50.3 us
    reshape x2, local copies, waits for them, and re-layouts, local(): image_tokens[asked.reshape(-1)].reshape(devices, capacity, image_len, model)  18.6 us
    dot_general x1, matrix products, attend(): jnp.einsum('bhqk,bkhd->bqhd', d_low, key_heads, preferred_element_type=jn...  15 us
    gather x1, local copies, waits for them, and re-layouts, local(): image_tokens[asked.reshape(-1)].reshape(devices, capacity, image_len, model)  15 us
    mul x2, local copies, waits for them, and re-layouts, attend(): weight_sum[..., None] * dir_heads[:, :, None, :]  13.4 us
    slice x2, local copies, waits for them, and re-layouts, attend(): keys_values[..., :model].reshape(count, image_len, HEADS, head_size)  12.9 us
  transfers between devices with their start and end apart: 3, of which 3 were waited for; matrix products, arithmetic and copies ran while one was open for 12% of the time, Pallas kernels for 0%

commit v1 on v0

v1 whole, which is shorter than its diff:
```python
import functools

import jax
import jax.numpy as jnp
import numpy as np
from jax import lax
from jax.experimental import pallas as pl
from jax.experimental.pallas import tpu as pltpu
from jax.sharding import PartitionSpec as P

HEADS = 12
PACK = 4
ROWS = 32
BF = jnp.bfloat16
F32 = jnp.float32
VMEM = pl.BlockSpec(memory_space=pltpu.VMEM)
SMEM = pl.BlockSpec(memory_space=pltpu.SMEM)
BIG = 56 * 1024 * 1024


def up(value, unit):
    return (value + unit - 1) // unit * unit


def nt(left, right):
    return lax.dot_general(left, right, (((1,), (1,)), ((), ())), preferred_element_type=F32)


def tn(left, right):
    return lax.dot_general(left, right, (((0,), (0,)), ((), ())), preferred_element_type=F32)


def nn(left, right):
    return jnp.dot(left, right, preferred_element_type=F32)


def keys_kernel(x_ref, w_ref, mh_ref, k_ref, u_ref, xp_ref):
    count, length, model = x_ref.shape
    head = model // HEADS
    gain = mh_ref[...]
    high = gain.astype(BF).astype(F32)
    middle = (gain - high).astype(BF).astype(F32)
    low = gain - high - middle
    rows = lax.broadcasted_iota(jnp.int32, (16, model), 0)
    lanes = lax.broadcasted_iota(jnp.int32, (16, model), 1)
    inside = (lanes >= rows * head) & (lanes < rows * head + head)
    parts = [jnp.where(inside, part, 0.0).astype(BF) for part in (high, middle, low)]
    for image in range(count):
        xp_ref[image] = jnp.zeros(xp_ref.shape[1:], BF)
        xp_ref[image, :length, :] = x_ref[image]
        rows_in = xp_ref[image]
        k_ref[image] = nn(rows_in, w_ref[:, :model]).astype(BF)
        values = nn(rows_in, w_ref[:, model:]).astype(BF)
        u_ref[image] = nt(parts[0], values) + nt(parts[1], values) + nt(parts[2], values)


def pairs_kernel(
    length, text_len, owner_ref, local_ref, tangent_ref, feat_k_ref, feat_q_ref, x_ref, k_ref,
    u_ref, t_ref, wq_ref, gk_ref, gq_ref, at_ref, lg_ref,
    tp_ref, q_ref, dk_ref, dq_ref, s_ref, text_s, col_s, image_s,
):
    count, padded, model = k_ref.shape
    head = model // HEADS
    width = PACK * head
    block = PACK * ROWS
    factor = head ** (-0.5)
    me = lax.axis_index("dev")
    requests = owner_ref.shape[0]
    real = lax.broadcasted_iota(jnp.int32, (ROWS, model), 0) < text_len

    def place(slot, text):
        rows = jnp.where(real, t_ref[text].astype(F32), 0.0).astype(BF)
        tp_ref[pl.ds(pl.multiple_of(slot * ROWS, ROWS), ROWS), :] = rows

    tp_ref[...] = jnp.zeros(tp_ref.shape, BF)
    dq_ref[...] = jnp.zeros(dq_ref.shape, BF)
    dk_ref[...] = jnp.zeros(dk_ref.shape, F32)
    s_ref[...] = jnp.zeros(s_ref.shape, F32)
    lg_ref[...] = jnp.zeros(lg_ref.shape, F32)
    for image in range(count):
        text_s[image] = me * count + image
        col_s[image] = 0
        image_s[image] = image
        place(image, me * count + image)

    def look(request, filled):
        mine = owner_ref[request] == me

        @pl.when(mine)
        def _():
            text = request // 2
            text_s[filled] = text
            col_s[filled] = request - 2 * text + 1
            image_s[filled] = local_ref[request]
            place(filled, text)

        return filled + mine.astype(jnp.int32)

    used = lax.fori_loop(0, requests, look, jnp.int32(count))
    q_ref[...] = nn(tp_ref[...], wq_ref[...]).astype(BF)

    row_head = lax.broadcasted_iota(jnp.int32, (block, width), 0) // ROWS
    lane_head = lax.broadcasted_iota(jnp.int32, (block, width), 1) // head
    diagonal = row_head == lane_head
    short_head = lax.broadcasted_iota(jnp.int32, (ROWS, width), 1) // head
    beyond = lax.broadcasted_iota(jnp.int32, (block, padded), 1) >= length
    sum_row = lax.broadcasted_iota(jnp.int32, (16, block), 0)
    sum_lane = lax.broadcasted_iota(jnp.int32, (16, block), 1)
    counted = (sum_lane // ROWS == sum_row) & (sum_lane % ROWS < text_len)
    summer = jnp.where(counted, 1.0, 0.0).astype(BF)

    def pair(slot, carry):
        image = image_s[slot]
        where = text_s[slot] * 3 + col_s[slot]
        scale = tangent_ref[where] / text_len
        rows = pl.ds(pl.multiple_of(slot * ROWS, ROWS), ROWS)
        total = jnp.zeros((1, padded), F32)
        for pack in range(HEADS // PACK):
            cols = slice(pack * width, (pack + 1) * width)
            four = q_ref[rows, cols].astype(F32)
            tall = jnp.concatenate([four] * PACK, axis=0)
            spread = jnp.where(diagonal, tall, 0.0).astype(BF)
            keys = k_ref[image, :, cols]
            scores = nt(spread, keys) * factor
            scores = jnp.where(beyond, -1e30, scores)
            scores = jnp.exp(scores - jnp.max(scores, axis=1, keepdims=True))
            probs = scores * (1.0 / jnp.sum(scores, axis=1, keepdims=True))
            weight_sum = nn(summer, probs.astype(BF))[:PACK]
            gains = u_ref[image, pack * PACK:(pack + 1) * PACK, :]
            total = total + jnp.sum(weight_sum * gains, axis=0, keepdims=True)
            s_ref[image, pack * PACK:(pack + 1) * PACK, :] += weight_sum * scale
            d_probs = jnp.concatenate(
                [jnp.broadcast_to(gains[h:h + 1], (ROWS, padded)) for h in range(PACK)], axis=0
            ) * scale
            centre = jnp.sum(probs * d_probs, axis=1, keepdims=True)
            d_low = (probs * (d_probs - centre)).astype(BF)
            dk_ref[image, :, cols] += tn(d_low, spread)
            wide = nn(d_low, keys)
            kept = jnp.zeros((ROWS, width), F32)
            for h in range(PACK):
                kept = jnp.where(short_head == h, wide[h * ROWS:(h + 1) * ROWS], kept)
            dq_ref[rows, cols] = (kept * factor).astype(BF)
        lg_ref[pl.ds(where, 1), :] = total * (1.0 / text_len)
        return carry

    lax.fori_loop(0, used, pair, 0)

    def one_hot(feat):
        lanes = lax.broadcasted_iota(jnp.int32, (feat.shape[0], model), 1)
        return jnp.where(lanes == feat, 1.0, 0.0).astype(BF)

    turn_q = one_hot(feat_q_ref[...])
    gq_ref[...] = nn(nt(turn_q, tp_ref[...]).astype(BF), dq_ref[...]).astype(gq_ref.dtype)
    turn_k = one_hot(feat_k_ref[...])
    for image in range(count):
        x_ref_rows = x_ref[image]
        flipped = nt(turn_k, x_ref_rows).astype(BF)
        part = nn(flipped, (dk_ref[image] * factor).astype(BF))
        weights = s_ref[image]
        high = weights.astype(BF)
        low = (weights - high.astype(F32)).astype(BF)
        sums = nn(high, x_ref_rows) + nn(low, x_ref_rows)
        if image == 0:
            gk_ref[...] = part
            at_ref[...] = sums
        else:
            gk_ref[...] += part
            at_ref[...] += sums


def feature_rows(model, total):
    return np.arange(model, dtype=np.int32)[:, None]


def local(image_tokens, text_tokens, negatives, query_weight, kv_weight, match_head, cotangent):
    count, length, model = image_tokens.shape
    text_len = text_tokens.shape[1]
    devices = lax.axis_size("dev")
    groups = lax.axis_size("grp")
    capacity = max(2, (2 * count + devices - 1) // devices)
    padded = up(length, 256)
    texts = devices * count
    slots = count + devices * capacity

    owner = negatives // count
    meta = jnp.concatenate(
        [cotangent, owner.astype(BF), (negatives - owner * count).astype(BF)], axis=1
    )
    meta = jnp.pad(meta, ((0, 0), (0, model - meta.shape[1])))[:, None, :]
    message = jnp.concatenate(
        [text_tokens, meta, jnp.zeros((count, ROWS - text_len - 1, model), BF)], axis=1
    )
    everyone = lax.all_gather(message, "dev", axis=0, tiled=True)

    keys, gains, pictures = pl.pallas_call(
        keys_kernel,
        out_shape=(
            jax.ShapeDtypeStruct((count, padded, model), BF),
            jax.ShapeDtypeStruct((count, 16, padded), F32),
            jax.ShapeDtypeStruct((count, padded, model), BF),
        ),
        in_specs=[VMEM] * 3,
        out_specs=(VMEM,) * 3,
        compiler_params=pltpu.CompilerParams(vmem_limit_bytes=BIG),
        cost_estimate=pl.CostEstimate(
            flops=4 * count * padded * model * model, bytes_accessed=8 * 1024 * 1024,
            transcendentals=0,
        ),
    )(image_tokens, kv_weight, match_head.reshape(1, model))

    facts = everyone[:, text_len, :8].astype(F32)
    owners = facts[:, 3:5].astype(jnp.int32).reshape(-1)
    locals_ = facts[:, 5:7].astype(jnp.int32).reshape(-1)
    tangents = facts[:, :3].reshape(-1)
    feat = feature_rows(model, groups * devices)
    span = feat.shape[0]
    grad_k, grad_q, sums, parts = pl.pallas_call(
        functools.partial(pairs_kernel, length, text_len),
        out_shape=(
            jax.ShapeDtypeStruct((span, model), F32),
            jax.ShapeDtypeStruct((span, model), BF),
            jax.ShapeDtypeStruct((16, model), F32),
            jax.ShapeDtypeStruct((texts * 3, padded), F32),
        ),
        in_specs=[SMEM] * 3 + [VMEM] * 7,
        out_specs=(VMEM,) * 4,
        scratch_shapes=[
            pltpu.VMEM((slots * ROWS, model), BF),
            pltpu.VMEM((slots * ROWS, model), BF),
            pltpu.VMEM((count, padded, model), F32),
            pltpu.VMEM((slots * ROWS, model), BF),
            pltpu.VMEM((count, 16, padded), F32),
            pltpu.SMEM((slots,), jnp.int32),
            pltpu.SMEM((slots,), jnp.int32),
            pltpu.SMEM((slots,), jnp.int32),
        ],
        compiler_params=pltpu.CompilerParams(vmem_limit_bytes=BIG),
        cost_estimate=pl.CostEstimate(
            flops=20 * 1024**3, bytes_accessed=16 * 1024 * 1024, transcendentals=0
        ),
    )(owners, locals_, tangents, feat, feat, pictures, keys, gains, everyone, query_weight)

    both = jnp.stack([grad_q, grad_k.astype(BF)], axis=1).reshape(span, 2 * model)
    grads = lax.psum_scatter(both, ("grp", "dev"), scatter_dimension=0, tiled=True).astype(F32)
    rows = model // (groups * devices)
    answers = jnp.sum(parts, axis=1).reshape(devices, count * 3)
    answers = jnp.where(
        jnp.arange(groups)[:, None, None] == lax.axis_index("grp"), answers[None], 0.0
    ).reshape(groups * devices, count * 3)
    factors = sums[:HEADS].T.reshape(groups * devices, rows * HEADS)
    small = lax.psum_scatter(
        jnp.concatenate([factors, answers], axis=1), ("grp", "dev"), scatter_dimension=0, tiled=True
    )
    logits = small[0, rows * HEADS:].reshape(count, 3)
    value_part = jnp.repeat(
        small[0, :rows * HEADS].reshape(rows, HEADS), model // HEADS, axis=1
    ) * match_head[None, :]
    return (
        logits, grads[:, :model], jnp.concatenate([grads[:, model:], value_part], axis=1)
    )


def solution(mesh):
    placed = (
        P(("grp", "dev"), None, None),
        P(("grp", "dev"), None, None),
        P(("grp", "dev"), None),
        P(),
        P(),
        P(),
        P(("grp", "dev"), None),
    )
    return jax.shard_map(
        local,
        mesh=mesh,
        in_specs=placed,
        out_specs=(P(("grp", "dev"), None), P(("grp", "dev"), None), P(("grp", "dev"), None)),
        check_vma=False,
    )
```

time: 485 us -> 206 us (0.42)
  waiting for transfers between devices: 258 us -> 73.5 us
  local copies, waits for them, and re-layouts: 122 us -> 17.9 us
  matrix products: 59 us -> 0 us
  Pallas kernels: 0 us -> 43 us
  blocking collectives: 11.7 us -> 51.5 us
  other arithmetic: 12.6 us -> 5.52 us
    reduce_scatter x1 -> x0, waiting for transfers between devices: 113 us -> none  [local(): lax.psum_scatter(grad_kv, ('grp', 'dev'), scatter_dimension=0, tiled=True)]
    all_to_all x1 -> x0, waiting for transfers between devices: 94.6 us -> none  [local(): lax.all_to_all(outgoing, 'dev', split_axis=0, concat_axis=0, tiled=True)]
    dot_general x8 -> x0, matrix products: 52.6 us -> none  [the longest x1 15 us: attend(): jnp.einsum('bhqk,bkhd->bqhd', d_low, key_heads, preferred_element_type=jn...]
    unnamed x0 -> x1, blocking collectives: none -> 51.5 us
    pallas_call x0 -> x2, Pallas kernels: none -> 43 us  [the longest x1 35.4 us: local(): pl.pallas_call(functools.partial(pairs_kernel, length, text_len), out_sha...]
    reshape x10 -> x6, local copies, waits for them, and re-layouts: 41.5 us -> 2.73 us  [the longest x1 0.64 us: local(): tangents = facts[:, :3].reshape(-1)]
    gather x2 -> x0, local copies, waits for them, and re-layouts: 19.6 us -> none  [the longest x1 15 us: local(): image_tokens[asked.reshape(-1)].reshape(devices, capacity, image_len, model)]
    slice x4, local copies, waits for them, and re-layouts: 19.4 us -> 0.31 us  [the longest x2 0.19 us: local(): grads[:, model:]]
  transfers between devices with their start and end apart: 3 -> 2, of which waited for: 3 -> 2; matrix products, arithmetic and copies ran while one was open for 12% -> 2% of each run, Pallas kernels for 0% -> 4%
where the time goes in v1:
time: 206 us
  waiting for transfers between devices  73.5 us (36%)
  blocking collectives  51.5 us (25%)
  Pallas kernels  43 us (21%)
  local copies, waits for them, and re-layouts  17.9 us (9%)
  between operations  14.2 us (7%)
  other arithmetic  5.52 us (3%)
    unnamed x3, waiting for transfers between devices  56.3 us
    unnamed x1, blocking collectives  51.5 us
    pallas_call x1, Pallas kernels, local(): pl.pallas_call(functools.partial(pairs_kernel, length, text_len), out_sha...  35.4 us
    all_gather x1, waiting for transfers between devices, local(): everyone = lax.all_gather(message, 'dev', axis=0, tiled=True)  17.2 us
    unnamed x14, local copies, waits for them, and re-layouts  11 us
    pallas_call x1, Pallas kernels, local(): pl.pallas_call(keys_kernel, out_shape=(jax.ShapeDtypeStruct((count, padde...  7.61 us
  transfers between devices with their start and end apart: 2, of which 2 were waited for; matrix products, arithmetic and copies ran while one was open for 2% of the time, Pallas kernels for 4%

profile of v1, /device:TPU:0, one launch (start us, length us, event | category | flops | bytes accessed | tf_op | source)
XLA Modules:
  0.0 205.6 jit_solution(7856521291502737067)
XLA Ops:
  7.2 0.0 all-gather.2.cloned.1.call-start
  7.2 0.8 copy.31
  8.0 0.8 fusion.5
  8.8 0.9 copy.36
  9.7 0.0 copy-start.3
  9.7 0.1 pad.13.clone
  9.8 0.8 maximum_maximum_fusion
  10.6 0.0 all-gather.2.cloned.1.call-update
  10.6 0.0 reduce-scatter.4.cloned.1.call-start
  10.6 2.4 %copy.38.x_ref = bf16[4,197,768]{2,1,0:T(8,128)(2,1)} copy(bf16[4,197,768]{2,0,1:T(4,128)(2,1)} %param.8) | data formatting | bytes 2420736 | tf_op args[0]
  13.1 0.0 copy-done.3
  13.1 0.6 reshape.42.mh_ref
  13.7 7.6 %shard_map.103 = (bf16[4,256,768]{2,1,0:T(8,128)(2,1)}, f32[4,16,256]{2,1,0:T(8,128)}, bf16[4,256,768]{2,1,0:T(8,128)(2,1)}) custom-call(bf16[4,197,768]{2,1,0:T(8,128)(2,1)} %copy.38.x_ref, bf16[768,1536]{1,0:T(8,128)(2,1)} %w_ref.1, f32[1,768]{1,0:T(1,128)} %reshape.42.mh_ref), custom_call_target="tpu_custom_call" | custom-call | flops 2415919104 | bytes 8388608 | tf_op jit(solution)/shard_map/pallas_call | solution.py:195
  21.3 17.2 %all-gather.2.cloned.1.call-done.t_ref = bf16[32,32,768]{2,1,0:T(8,128)(2,1)} async-done(((bf16[4,32,768]{2,1,0:T(8,128)(2,1)}), bf16[32,32,768]{2,1,0:T(8,128)(2,1)}) %all-gather.2.cloned.1.call-update) | async-done | bytes 1572880 | tf_op jit(solution)/shard_map/all_gather | solution.py:193
  38.5 0.9 slice_convert_fusion.2
  39.4 0.1 slice_convert_fusion
  39.4 0.6 reshape.39.owner_ref
  40.1 0.6 reshape.40.local_ref
  40.7 0.6 reshape.41.tangent_ref
  41.3 35.4 %shard_map.104 = (f32[768,768]{1,0:T(8,128)}, bf16[768,768]{1,0:T(8,128)(2,1)}, f32[16,768]{1,0:T(8,128)}, f32[96,256]{1,0:T(8,128)}) custom-call(s32[64]{0:T(128)} %reshape.39.owner_ref, s32[64]{0:T(128)} %reshape.40.local_ref, f32[96]{0:T(128)} %reshape.41.tangent_ref, s32[768,1]{1,0:T(8,128)} %constant.31.clone.feat_k_ref.feat_q_ref, ...), custom_call_target="tpu_custom_call" | custom-call | flops 21474836480 | bytes 16777216 | tf_op jit(solution)/shard_map/pallas_call | solution.py:217
  76.7 0.0 copy-start
  76.7 1.9 convert_bitcast_fusion
  78.6 0.1 copy-done
  78.7 0.2 pad_maximum_fusion
  78.9 2.5 %copy.40 = bf16[768,2,768]{0,2,1:T(8,128)(2,1)} copy(bf16[768,2,768]{2,0,1:T(8,128)(2,1)S(1)} %pad_maximum_fusion) | data formatting | bytes 4718592 | tf_op jit(solution)/shard_map/stack | solution.py:243
  81.4 4.3 %copy.43 = bf16[768,1536]{1,0:T(8,128)(2,1)} copy(bf16[768,1536]{0,1:T(8,128)(2,1)} %bitcast.14) | data formatting | bytes 4718592
  85.7 0.0 copy-start.2
  85.7 0.0 copy-start.1
  85.7 0.0 reduce-scatter.4.cloned.1.call-update
  85.7 0.1 broadcast_in_dim.41
  85.8 0.1 broadcast_in_dim.42
  85.9 0.6 copy-done.2
  86.5 0.2 copy.39
  86.7 0.2 reshape.43
  86.8 0.0 copy-done.1
  86.8 0.1 reduce_sum.9
  87.0 0.1 broadcast_in_dim.44
  87.0 0.1 bitcast_select_fusion
  87.1 0.1 pad_maximum_fusion.2
  87.2 51.5 %all-reduce.1 = f32[32,300]{1,0:T(8,128)S(1)} all-reduce(f32[32,300]{1,0:T(8,128)S(1)} %pad_maximum_fusion.2), channel_id=2, replica_groups=mesh['grp'=4,'dev'=8] {'grp','dev'}, use_global_device_ids=true, to_apply=%region_1.2.clone | all-reduce | flops 9600 | bytes 76800
  138.7 0.1 reshape_squeeze.7
  138.8 0.1 broadcast_in_dim.48
  138.9 0.1 reshape.45
  139.0 0.1 dynamic-slice_reduce_fusion.1
  139.1 0.7 reshape_squeeze.6
  139.8 56.2 %reduce-scatter.4.cloned.1.call-done = bf16[24,1536]{1,0:T(8,128)(2,1)} async-done(((bf16[768,1536]{1,0:T(8,128)(2,1)}), bf16[24,1536]{1,0:T(8,128)(2,1)}) %reduce-scatter.4.cloned.1.call-update) | async-done | bytes 73744
  196.0 1.1 copy.44
  197.1 0.1 fusion.9
  197.2 0.1 copy.41
  197.3 0.8 copy.42
  198.1 0.7 pad_maximum_fusion.1
  (6 shorter events, 0.1 us)
Async XLA Ops:
  7.2 31.3 %all-gather.2.cloned.1.call-start = ((), (), s32[]{:S(2)}) async-start(), calls=%async_computation.1 | async-start | bytes 1769472 | tf_op jit(solution)/shard_map/all_gather | solution.py:193
  9.7 3.4 %copy-start.3 = (f32[768]{0:T(1024)S(1)}, f32[768]{0:T(1024)}, u32[]{:S(2)}) copy-start(f32[768]{0:T(1024)} %param.13) | copy-start | bytes 9220
  10.6 185.4 %reduce-scatter.4.cloned.1.call-start = ((), (), s32[]{:S(2)}) async-start(), calls=%async_computation.2 | async-start | bytes 2433024
  76.7 2.0 copy-start
  85.7 0.8 copy-start.2
  85.7 1.2 copy-start.1
Sparse Core Ops, SparseCore 0:
  10.7 27.7 all-gather.1
  85.8 110.1 reduce-scatter.3

commit v2 on v1

--- a/solution.py
+++ b/solution.py
@@ -55,9 +55,9 @@
 
 
 def pairs_kernel(
-    length, text_len, owner_ref, local_ref, tangent_ref, feat_k_ref, feat_q_ref, x_ref, k_ref,
-    u_ref, t_ref, wq_ref, gk_ref, gq_ref, at_ref, lg_ref,
-    tp_ref, q_ref, dk_ref, dq_ref, s_ref, text_s, col_s, image_s,
+    length, text_len, owner_ref, local_ref, tangent_ref, feat_k_ref, feat_q_ref, home_ref, x_ref,
+    k_ref, u_ref, t_ref, wq_ref, gk_ref, gq_ref, small_ref,
+    tp_ref, q_ref, dk_ref, dq_ref, s_ref, lg_ref, text_s, col_s, image_s,
 ):
     count, padded, model = k_ref.shape
     head = model // HEADS
@@ -149,27 +149,173 @@
         lanes = lax.broadcasted_iota(jnp.int32, (feat.shape[0], model), 1)
         return jnp.where(lanes == feat, 1.0, 0.0).astype(BF)
 
+    blocks, tall_rows, half = gq_ref.shape
+    lines = tall_rows // 2
+
+    def store(out_ref, left, right):
+        sides = [
+            nn(left, right[:, side * half:(side + 1) * half]).reshape(blocks, lines, half)
+            for side in range(2)
+        ]
+        out_ref[...] = jnp.concatenate(sides, axis=1).astype(BF)
+
     turn_q = one_hot(feat_q_ref[...])
-    gq_ref[...] = nn(nt(turn_q, tp_ref[...]).astype(BF), dq_ref[...]).astype(gq_ref.dtype)
+    store(gq_ref, nt(turn_q, tp_ref[...]).astype(BF), dq_ref[...])
     turn_k = one_hot(feat_k_ref[...])
+    pictures = x_ref[...].reshape(count * padded, model)
+    flipped = nt(turn_k, pictures).astype(BF)
+    store(gk_ref, flipped, (dk_ref[...] * factor).astype(BF).reshape(count * padded, model))
+
+    answers = jnp.sum(lg_ref[...], axis=1, keepdims=True)
+    outs = answers.shape[0]
+    lane = lax.broadcasted_iota(jnp.int32, (outs, 128), 1)
+    line = lax.broadcasted_iota(jnp.int32, (outs, 128), 0)
+    rest = jnp.where(lane - 16 == line % (3 * count), answers, 0.0)
+    homes = lax.broadcasted_iota(jnp.int32, (blocks * lines, outs), 0) == home_ref[...]
+    homes = jnp.where(homes, 1.0, 0.0).astype(BF)
+    small = jnp.zeros((blocks * lines, 128), F32)
+    for step in range(3):
+        piece = rest.astype(BF)
+        rest = rest - piece.astype(F32)
+        small = small + nn(homes, piece)
     for image in range(count):
-        x_ref_rows = x_ref[image]
-        flipped = nt(turn_k, x_ref_rows).astype(BF)
-        part = nn(flipped, (dk_ref[image] * factor).astype(BF))
         weights = s_ref[image]
         high = weights.astype(BF)
         low = (weights - high.astype(F32)).astype(BF)
-        sums = nn(high, x_ref_rows) + nn(low, x_ref_rows)
-        if image == 0:
-            gk_ref[...] = part
-            at_ref[...] = sums
+        mine = flipped[:, image * padded:(image + 1) * padded]
+        small = small + nt(mine, high) + nt(mine, low)
+    small_ref[...] = small.reshape(blocks, lines, 128)
+
+
+def reduce_kernel(
+    rows, orders, k_ref, q_ref, small_ref, mh_ref, gq_ref, gkv_ref, logit_ref,
+    k_acc, q_acc, s_acc, k_send, q_send, s_send, k_recv, q_recv, s_recv, send_sem, recv_sem,
+):
+    devices = lax.axis_size("dev")
+    me = lax.axis_index("grp") * devices + lax.axis_index("dev")
+    blocks = k_ref.shape[0]
+    steps = len(orders[0])
+
+    def bit_of(bit):
+        return lax.rem(lax.div(me, 1 << bit), 2)
+
+    def partner(bit):
+        other = me + (1 - 2 * bit_of(bit)) * (1 << bit)
+        return (lax.div(other, devices), lax.rem(other, devices))
+
+    barrier = pltpu.get_barrier_semaphore()
+    for bit in range(steps):
+        pl.semaphore_signal(
+            barrier, inc=1, device_id=partner(bit), device_id_type=pl.DeviceIdType.MESH
+        )
+    pl.semaphore_wait(barrier, steps)
+
+    streams = (
+        (k_ref, k_acc, k_send, k_recv, orders[0]),
+        (q_ref, q_acc, q_send, q_recv, orders[1]),
+        (small_ref, s_acc, s_send, s_recv, orders[0]),
+    )
+    copies = {}
+
+    def send(index, step):
+        source, acc, staged, landed, order = streams[index]
+        size = blocks >> (step + 1)
+        base = blocks - 2 * size
+        away = (1 - bit_of(order[step])) * size
+        if step == 0:
+            held = source.at[pl.ds(away, size)]
         else:
-            gk_ref[...] += part
-            at_ref[...] += sums
-
-
-def feature_rows(model, total):
-    return np.arange(model, dtype=np.int32)[:, None]
+            lower = base - blocks // 2
+            held = staged.at[pl.ds(lower, size)]
+            staged[pl.ds(lower, size)] = acc[pl.ds(start_of(order, step) + away, size)].astype(
+                staged.dtype
+            )
+        copies[index, step] = pltpu.make_async_remote_copy(
+            src_ref=held,
+            dst_ref=landed.at[pl.ds(base, size)],
+            send_sem=send_sem.at[index, step],
+            recv_sem=recv_sem.at[index, step],
+            device_id=partner(order[step]),
+            device_id_type=pl.DeviceIdType.MESH,
+        )
+        copies[index, step].start()
+
+    def start_of(order, step):
+        start = 0
+        for earlier in range(1, step):
+            start = start + bit_of(order[earlier]) * (blocks >> (earlier + 1))
+        return start
+
+    def add(index, step):
+        source, acc, staged, landed, order = streams[index]
+        size = blocks >> (step + 1)
+        base = blocks - 2 * size
+        copies[index, step].wait_recv()
+        arrived = landed[pl.ds(base, size)].astype(F32)
+        keep = bit_of(order[step]) * size
+        if step == 0:
+            acc[...] = source[pl.ds(keep, size)].astype(F32) + arrived
+        else:
+            spot = pl.ds(start_of(order, step) + keep, size)
+            acc[spot] = acc[spot] + arrived
+
+    for index in range(3):
+        send(index, 0)
+    for step in range(steps):
+        for index in range(3):
+            add(index, step)
+            if step + 1 < steps:
+                send(index, step + 1)
+    for step in range(steps):
+        for index in range(3):
+            copies[index, step].wait_send()
+
+    lines = k_ref.shape[1] // 2
+    half = k_ref.shape[2]
+    model = 2 * half
+    head = model // HEADS
+    k_sum = k_acc[pl.ds(start_of(orders[0], steps), 1)][0]
+    q_sum = q_acc[pl.ds(start_of(orders[1], steps), 1)][0]
+    s_sum = s_acc[pl.ds(start_of(orders[0], steps), 1)][0]
+    logit_ref[...] = s_sum[:8]
+    lane_head = lax.broadcasted_iota(jnp.int32, (128, model), 1) // head
+    open_up = lax.broadcasted_iota(jnp.int32, (128, model), 0) == lane_head
+    open_up = jnp.where(open_up, 1.0, 0.0).astype(BF)
+    value = jnp.zeros((lines, model), F32)
+    rest = s_sum
+    for step in range(3):
+        piece = rest.astype(BF)
+        rest = rest - piece.astype(F32)
+        value = value + nn(piece, open_up)
+    value = value * mh_ref[...]
+    gq_ref[:, :half] = q_sum[:rows]
+    gq_ref[:, half:] = q_sum[lines:lines + rows]
+    gkv_ref[:, :half] = k_sum[:rows]
+    gkv_ref[:, half:model] = k_sum[lines:lines + rows]
+    gkv_ref[:, model:] = value[:rows]
+
+
+def bit_orders(groups, devices):
+    low = devices.bit_length() - 1
+    across = list(range(low, low + groups.bit_length() - 1))
+    along = list(range(1, low))
+    return (0, *across, *along), (0, *reversed(across), *along)
+
+
+def places(total, order):
+    at = np.arange(total)
+    owner = np.zeros(total, np.int32)
+    for step, bit in enumerate(order):
+        owner |= ((at >> (len(order) - 1 - step)) & 1) << bit
+    return owner
+
+
+def feature_rows(model, total, order):
+    rows = model // total
+    lines = up(rows, 8)
+    line = np.arange(lines)[None, :]
+    feat = np.where(line < rows, places(total, order)[:, None] * rows + line, -1)
+    return feat.reshape(-1, 1).astype(np.int32)
 
 
 def local(image_tokens, text_tokens, negatives, query_weight, kv_weight, match_head, cotangent):
@@ -212,24 +358,31 @@
     owners = facts[:, 3:5].astype(jnp.int32).reshape(-1)
     locals_ = facts[:, 5:7].astype(jnp.int32).reshape(-1)
     tangents = facts[:, :3].reshape(-1)
-    feat = feature_rows(model, groups * devices)
-    span = feat.shape[0]
-    grad_k, grad_q, sums, parts = pl.pallas_call(
+    total = groups * devices
+    rows = model // total
+    lines = up(rows, 8)
+    half = model // 2
+    orders = bit_orders(groups, devices)
+    feat_k, feat_q = (feature_rows(model, total, order) for order in orders)
+    home = np.argsort(places(total, orders[0])).astype(np.int32) * lines
+    home = np.repeat(home, count * 3).reshape(groups, 1, texts * 3)
+    home = lax.dynamic_index_in_dim(jnp.asarray(home), lax.axis_index("grp"), 0, keepdims=False)
+    grad_k, grad_q, small = pl.pallas_call(
         functools.partial(pairs_kernel, length, text_len),
         out_shape=(
-            jax.ShapeDtypeStruct((span, model), F32),
-            jax.ShapeDtypeStruct((span, model), BF),
-            jax.ShapeDtypeStruct((16, model), F32),
-            jax.ShapeDtypeStruct((texts * 3, padded), F32),
-        ),
-        in_specs=[SMEM] * 3 + [VMEM] * 7,
-        out_specs=(VMEM,) * 4,
+            jax.ShapeDtypeStruct((total, 2 * lines, half), BF),
+            jax.ShapeDtypeStruct((total, 2 * lines, half), BF),
+            jax.ShapeDtypeStruct((total, lines, 128), F32),
+        ),
+        in_specs=[SMEM] * 3 + [VMEM] * 8,
+        out_specs=(VMEM,) * 3,
         scratch_shapes=[
             pltpu.VMEM((slots * ROWS, model), BF),
             pltpu.VMEM((slots * ROWS, model), BF),
             pltpu.VMEM((count, padded, model), F32),
             pltpu.VMEM((slots * ROWS, model), BF),
-            pltpu.VMEM((count, 16, padded), F32),
+            pltpu.VMEM((count, 128, padded), F32),
+            pltpu.VMEM((texts * 3, padded), F32),
             pltpu.SMEM((slots,), jnp.int32),
             pltpu.SMEM((slots,), jnp.int32),
             pltpu.SMEM((slots,), jnp.int32),
@@ -238,26 +391,41 @@
         cost_estimate=pl.CostEstimate(
             flops=20 * 1024**3, bytes_accessed=16 * 1024 * 1024, transcendentals=0
         ),
-    )(owners, locals_, tangents, feat, feat, pictures, keys, gains, everyone, query_weight)
-
-    both = jnp.stack([grad_q, grad_k.astype(BF)], axis=1).reshape(span, 2 * model)
-    grads = lax.psum_scatter(both, ("grp", "dev"), scatter_dimension=0, tiled=True).astype(F32)
-    rows = model // (groups * devices)
-    answers = jnp.sum(parts, axis=1).reshape(devices, count * 3)
-    answers = jnp.where(
-        jnp.arange(groups)[:, None, None] == lax.axis_index("grp"), answers[None], 0.0
-    ).reshape(groups * devices, count * 3)
-    factors = sums[:HEADS].T.reshape(groups * devices, rows * HEADS)
-    small = lax.psum_scatter(
-        jnp.concatenate([factors, answers], axis=1), ("grp", "dev"), scatter_dimension=0, tiled=True
-    )
-    logits = small[0, rows * HEADS:].reshape(count, 3)
-    value_part = jnp.repeat(
-        small[0, :rows * HEADS].reshape(rows, HEADS), model // HEADS, axis=1
-    ) * match_head[None, :]
-    return (
-        logits, grads[:, :model], jnp.concatenate([grads[:, model:], value_part], axis=1)
-    )
+    )(owners, locals_, tangents, feat_k, feat_q, home, pictures, keys, gains, everyone,
+      query_weight)
+
+    steps = len(orders[0])
+    grad_query, grad_kv, answers = pl.pallas_call(
+        functools.partial(reduce_kernel, rows, orders),
+        out_shape=(
+            jax.ShapeDtypeStruct((rows, model), F32),
+            jax.ShapeDtypeStruct((rows, 2 * model), F32),
+            jax.ShapeDtypeStruct((8, 128), F32),
+        ),
+        in_specs=[VMEM] * 4,
+        out_specs=(VMEM,) * 3,
+        scratch_shapes=[
+            pltpu.VMEM((total // 2, 2 * lines, half), F32),
+            pltpu.VMEM((total // 2, 2 * lines, half), F32),
+            pltpu.VMEM((total // 2, lines, 128), F32),
+            pltpu.VMEM((total // 2, 2 * lines, half), BF),
+            pltpu.VMEM((total // 2, 2 * lines, half), BF),
+            pltpu.VMEM((total // 2, lines, 128), F32),
+            pltpu.VMEM((total, 2 * lines, half), BF),
+            pltpu.VMEM((total, 2 * lines, half), BF),
+            pltpu.VMEM((total, lines, 128), F32),
+            pltpu.SemaphoreType.DMA((3, steps)),
+            pltpu.SemaphoreType.DMA((3, steps)),
+        ],
+        compiler_params=pltpu.CompilerParams(
+            vmem_limit_bytes=40 * 1024 * 1024, collective_id=0, has_side_effects=True
+        ),
+        cost_estimate=pl.CostEstimate(
+            flops=1024**2, bytes_accessed=8 * 1024 * 1024, transcendentals=0
+        ),
+    )(grad_k, grad_q, small, match_head.reshape(1, model))
+    logits = answers[0, 16:16 + 3 * count].reshape(count, 3)
+    return (logits, grad_query, grad_kv)
 
 
 def solution(mesh):

time: 206 us -> 128 us (0.62)
  waiting for transfers between devices: 73.5 us -> 15.4 us
  blocking collectives: 51.5 us -> 0 us
  Pallas kernels: 43 us -> 80.7 us
  local copies, waits for them, and re-layouts: 17.9 us -> 14.2 us
  other arithmetic: 5.52 us -> 2.49 us
    unnamed x3 -> x1, waiting for transfers between devices: 56.3 us -> 0.02 us
    unnamed x1 -> x0, blocking collectives: 51.5 us -> none
    pallas_call x0 -> x1, Pallas kernels: none -> 44.2 us  [local(): pl.pallas_call(functools.partial(reduce_kernel, rows, orders), out_shape=...]
    pallas_call x1, Pallas kernels: 35.4 us -> 29 us  [local(): pl.pallas_call(functools.partial(pairs_kernel, length, text_len), out_sha...]
    another operation x3 -> x1, local copies, waits for them, and re-layouts: 3.22 us -> 0.66 us  [local(): logits = answers[0, 16:16 + 3 * count].reshape(count, 3)]
    another operation x2 -> x0, other arithmetic: 2.09 us -> none  [local(): jnp.stack([grad_q, grad_k.astype(BF)], axis=1).reshape(span, 2 * model)]
    unnamed x14 -> x13, local copies, waits for them, and re-layouts: 11 us -> 9.03 us
  transfers between devices with their start and end apart: 2 -> 1, of which waited for: 2 -> 1; matrix products, arithmetic and copies ran while one was open for 2% -> 4% of each run, Pallas kernels for 4% -> 6%
where the time goes in v2:
time: 128 us; the launch traced here: 127 us
  Pallas kernels  80.7 us (63%)
  waiting for transfers between devices  15.4 us (12%)
  local copies, waits for them, and re-layouts  14.2 us (11%)
  between operations  14.1 us (11%)
  other arithmetic  2.49 us (2%)
    pallas_call x1, Pallas kernels, local(): pl.pallas_call(functools.partial(reduce_kernel, rows, orders), out_shape=...  44.2 us
    pallas_call x1, Pallas kernels, local(): pl.pallas_call(functools.partial(pairs_kernel, length, text_len), out_sha...  29 us
    all_gather x1, waiting for transfers between devices, local(): everyone = lax.all_gather(message, 'dev', axis=0, tiled=True)  15.4 us
    unnamed x13, local copies, waits for them, and re-layouts  9.03 us
    pallas_call x1, Pallas kernels, local(): pl.pallas_call(keys_kernel, out_shape=(jax.ShapeDtypeStruct((count, padde...  7.59 us
  transfers between devices with their start and end apart: 1, of which 1 were waited for; matrix products, arithmetic and copies ran while one was open for 4% of the time, Pallas kernels for 6%

profile of v2, /device:TPU:0, one launch (start us, length us, event | category | flops | bytes accessed | tf_op | source)
XLA Modules:
  0.0 126.9 jit_solution(16940265086867228597)
XLA Ops:
  7.2 0.0 all-gather.2.cloned.1.call-start
  7.2 0.8 copy.28
  8.0 0.8 fusion.5
  8.8 0.9 copy.33
  9.7 0.1 pad.7.clone
  9.8 0.8 maximum_maximum_fusion
  10.6 0.0 all-gather.2.cloned.1.call-update
  10.6 1.3 reshape.24.mh_ref
  11.9 2.5 %copy.35.x_ref = bf16[4,197,768]{2,1,0:T(8,128)(2,1)} copy(bf16[4,197,768]{2,0,1:T(4,128)(2,1)} %param.10) | data formatting | bytes 2420736 | tf_op args[0]
  14.4 1.2 dynamic-slice_bitcast_fusion.home_ref
  15.6 7.6 %shard_map.121 = (bf16[4,256,768]{2,1,0:T(8,128)(2,1)}, f32[4,16,256]{2,1,0:T(8,128)}, bf16[4,256,768]{2,1,0:T(8,128)(2,1)}) custom-call(bf16[4,197,768]{2,1,0:T(8,128)(2,1)} %copy.35.x_ref, bf16[768,1536]{1,0:T(8,128)(2,1)} %w_ref.1, f32[1,768]{1,0:T(1,128)} %reshape.24.mh_ref), custom_call_target="tpu_custom_call" | custom-call | flops 2415919104 | bytes 8388608 | tf_op jit(solution)/shard_map/pallas_call | solution.py:341
  23.2 15.4 %all-gather.2.cloned.1.call-done.t_ref = bf16[32,32,768]{2,1,0:T(8,128)(2,1)} async-done(((bf16[4,32,768]{2,1,0:T(8,128)(2,1)}), bf16[32,32,768]{2,1,0:T(8,128)(2,1)}) %all-gather.2.cloned.1.call-update) | async-done | bytes 1572880 | tf_op jit(solution)/shard_map/all_gather | solution.py:339
  38.5 0.9 slice_convert_fusion.2
  39.4 0.1 slice_convert_fusion
  39.5 0.7 reshape.23.tangent_ref
  40.1 0.6 reshape.22.local_ref
  40.7 0.6 reshape.21.owner_ref
  41.4 0.0 copy-start.3
  41.4 29.0 %shard_map.122 = (bf16[32,48,384]{2,1,0:T(8,128)(2,1)}, bf16[32,48,384]{2,1,0:T(8,128)(2,1)}, f32[32,24,128]{2,1,0:T(8,128)}) custom-call(s32[64]{0:T(128)} %reshape.21.owner_ref, s32[64]{0:T(128)} %reshape.22.local_ref, f32[96]{0:T(128)} %reshape.23.tangent_ref, s32[768,1]{1,0:T(8,128)} %constant.38.clone.feat_k_ref, s32[768,1]{1,0:T(8,128)} %constant.39.clone.feat_q_ref, ...), custom_call_target="tpu_custom_call" | custom-call | flops 21474836480 | bytes 16777216 | tf_op jit(solution)/shard_map/pallas_call | solution.py:370
  70.3 0.0 copy-done.3
  70.3 0.0 copy-start
  70.3 1.3 copy-done
  71.6 0.0 copy-start.1
  71.6 1.3 copy-done.1
  72.9 0.0 copy-start.2
  72.9 1.0 copy-done.2
  73.9 44.2 %shard_map.123 = (f32[24,768]{1,0:T(8,128)S(1)}, f32[24,1536]{1,0:T(8,128)S(1)}, f32[8,128]{1,0:T(8,128)S(1)}) custom-call(bf16[32,48,384]{2,1,0:T(8,128)(2,1)S(1)} %copy-done, bf16[32,48,384]{2,1,0:T(8,128)(2,1)S(1)} %copy-done.1, f32[32,24,128]{2,1,0:T(8,128)S(1)} %copy-done.2, f32[1,768]{1,0:T(1,128)S(1)} %copy-done.3), custom_call_target="tpu_custom_call" | custom-call | flops 1048576 | bytes 8388608 | tf_op jit(solution)/shard_map/pallas_call | solution.py:398
  118.1 0.1 slice_reduce_fusion
  118.1 0.7 reshape_squeeze.3
  118.8 0.6 copy.38
  119.4 0.7 copy.39
  (2 shorter events, 0.0 us)
Async XLA Ops:
  7.2 31.4 %all-gather.2.cloned.1.call-start = ((), (), s32[]{:S(2)}) async-start(), calls=%async_computation | async-start | bytes 1769472 | tf_op jit(solution)/shard_map/all_gather | solution.py:339
  41.4 29.0 %copy-start.3 = (f32[1,768]{1,0:T(1,128)S(1)}, f32[1,768]{1,0:T(1,128)}, u32[]{:S(2)}) copy-start(f32[1,768]{1,0:T(1,128)} %reshape.24.mh_ref) | copy-start | bytes 9220
  70.3 1.3 %copy-start = (bf16[32,48,384]{2,1,0:T(8,128)(2,1)S(1)}, bf16[32,48,384]{2,1,0:T(8,128)(2,1)}, u32[]{:S(2)}) copy-start(bf16[32,48,384]{2,1,0:T(8,128)(2,1)} %get-tuple-element.15.k_ref) | copy-start | bytes 3538948
  71.6 1.3 %copy-start.1 = (bf16[32,48,384]{2,1,0:T(8,128)(2,1)S(1)}, bf16[32,48,384]{2,1,0:T(8,128)(2,1)}, u32[]{:S(2)}) copy-start(bf16[32,48,384]{2,1,0:T(8,128)(2,1)} %get-tuple-element.16.q_ref) | copy-start | bytes 3538948
  72.9 1.0 copy-start.2
Sparse Core Ops, SparseCore 0:
  10.7 27.7 all-gather.1

commit v3 on v2

--- a/solution.py
+++ b/solution.py
@@ -34,7 +34,12 @@
     return jnp.dot(left, right, preferred_element_type=F32)
 
 
-def keys_kernel(x_ref, w_ref, mh_ref, k_ref, u_ref, xp_ref):
+def one_hot(feat, model):
+    lanes = lax.broadcasted_iota(jnp.int32, (feat.shape[0], model), 1)
+    return jnp.where(lanes == feat, 1.0, 0.0).astype(BF)
+
+
+def keys_kernel(x_ref, w_ref, mh_ref, feat_ref, k_ref, u_ref, flip_ref, xp_ref):
     count, length, model = x_ref.shape
     head = model // HEADS
     gain = mh_ref[...]
@@ -45,17 +50,20 @@
     lanes = lax.broadcasted_iota(jnp.int32, (16, model), 1)
     inside = (lanes >= rows * head) & (lanes < rows * head + head)
     parts = [jnp.where(inside, part, 0.0).astype(BF) for part in (high, middle, low)]
+    turn = one_hot(feat_ref[...], model)
     for image in range(count):
         xp_ref[image] = jnp.zeros(xp_ref.shape[1:], BF)
         xp_ref[image, :length, :] = x_ref[image]
         rows_in = xp_ref[image]
+        padded = rows_in.shape[0]
+        flip_ref[:, image * padded:(image + 1) * padded] = nt(turn, rows_in).astype(BF)
         k_ref[image] = nn(rows_in, w_ref[:, :model]).astype(BF)
         values = nn(rows_in, w_ref[:, model:]).astype(BF)
         u_ref[image] = nt(parts[0], values) + nt(parts[1], values) + nt(parts[2], values)
 
 
 def pairs_kernel(
-    length, text_len, owner_ref, local_ref, tangent_ref, feat_k_ref, feat_q_ref, home_ref, x_ref,
+    length, text_len, owner_ref, local_ref, tangent_ref, feat_q_ref, home_ref, flip_ref,
     k_ref, u_ref, t_ref, wq_ref, gk_ref, gq_ref, small_ref,
     tp_ref, q_ref, dk_ref, dq_ref, s_ref, lg_ref, text_s, col_s, image_s,
 ):
@@ -66,6 +74,11 @@
     factor = head ** (-0.5)
     me = lax.axis_index("dev")
     requests = owner_ref.shape[0]
+    outs = tangent_ref.shape[0]
+    for slot in range(text_s.shape[0]):
+        text_s[slot] = 0
+        col_s[slot] = 0
+        image_s[slot] = 0
     real = lax.broadcasted_iota(jnp.int32, (ROWS, model), 0) < text_len
 
     def place(slot, text):
@@ -109,45 +122,63 @@
     counted = (sum_lane // ROWS == sum_row) & (sum_lane % ROWS < text_len)
     summer = jnp.where(counted, 1.0, 0.0).astype(BF)
 
-    def pair(slot, carry):
-        image = image_s[slot]
-        where = text_s[slot] * 3 + col_s[slot]
-        scale = tangent_ref[where] / text_len
-        rows = pl.ds(pl.multiple_of(slot * ROWS, ROWS), ROWS)
-        total = jnp.zeros((1, padded), F32)
-        for pack in range(HEADS // PACK):
-            cols = slice(pack * width, (pack + 1) * width)
-            four = q_ref[rows, cols].astype(F32)
+    together = 2
+
+    def pairs(turn, carry):
+        slots = [turn * together + extra for extra in range(together)]
+        images = [image_s[slot] for slot in slots]
+        wheres = [text_s[slot] * 3 + col_s[slot] for slot in slots]
+        scales = [
+            jnp.where(slot < used, tangent_ref[where], 0.0) / text_len
+            for slot, where in zip(slots, wheres)
+        ]
+        rows = [pl.ds(pl.multiple_of(slot * ROWS, ROWS), ROWS) for slot in slots]
+        jobs = [(each, pack) for each in range(together) for pack in range(HEADS // PACK)]
+        cols = [slice(pack * width, (pack + 1) * width) for _, pack in jobs]
+        spreads, keys, probs, weights, gains, lows = [], [], [], [], [], []
+        for job, (each, pack) in enumerate(jobs):
+            four = q_ref[rows[each], cols[job]].astype(F32)
             tall = jnp.concatenate([four] * PACK, axis=0)
-            spread = jnp.where(diagonal, tall, 0.0).astype(BF)
-            keys = k_ref[image, :, cols]
-            scores = nt(spread, keys) * factor
-            scores = jnp.where(beyond, -1e30, scores)
-            scores = jnp.exp(scores - jnp.max(scores, axis=1, keepdims=True))
-            probs = scores * (1.0 / jnp.sum(scores, axis=1, keepdims=True))
-            weight_sum = nn(summer, probs.astype(BF))[:PACK]
-            gains = u_ref[image, pack * PACK:(pack + 1) * PACK, :]
-            total = total + jnp.sum(weight_sum * gains, axis=0, keepdims=True)
-            s_ref[image, pack * PACK:(pack + 1) * PACK, :] += weight_sum * scale
+            spreads.append(jnp.where(diagonal, tall, 0.0).astype(BF))
+            keys.append(k_ref[images[each], :, cols[job]])
+            gains.append(u_ref[images[each], pack * PACK:(pack + 1) * PACK, :])
+        scores = [nt(spread, key) for spread, key in zip(spreads, keys)]
+        for score in scores:
+            score = jnp.where(beyond, -1e30, score * factor)
+            score = jnp.exp(score - jnp.max(score, axis=1, keepdims=True))
+            probs.append(score * (1.0 / jnp.sum(score, axis=1, keepdims=True)))
+        for job, (each, pack) in enumerate(jobs):
+            weights.append(nn(summer, probs[job].astype(BF))[:PACK])
             d_probs = jnp.concatenate(
-                [jnp.broadcast_to(gains[h:h + 1], (ROWS, padded)) for h in range(PACK)], axis=0
-            ) * scale
-            centre = jnp.sum(probs * d_probs, axis=1, keepdims=True)
-            d_low = (probs * (d_probs - centre)).astype(BF)
-            dk_ref[image, :, cols] += tn(d_low, spread)
-            wide = nn(d_low, keys)
+                [
+                    jnp.broadcast_to(gains[job][h:h + 1] * scales[each], (ROWS, padded))
+                    for h in range(PACK)
+                ],
+                axis=0,
+            )
+            centre = jnp.sum(probs[job] * d_probs, axis=1, keepdims=True)
+            lows.append((probs[job] * (d_probs - centre)).astype(BF))
+        d_keys = [tn(low, spread) for low, spread in zip(lows, spreads)]
+        wides = [nn(low, key) for low, key in zip(lows, keys)]
+        for job, (each, pack) in enumerate(jobs):
             kept = jnp.zeros((ROWS, width), F32)
             for h in range(PACK):
-                kept = jnp.where(short_head == h, wide[h * ROWS:(h + 1) * ROWS], kept)
-            dq_ref[rows, cols] = (kept * factor).astype(BF)
-        lg_ref[pl.ds(where, 1), :] = total * (1.0 / text_len)
+                kept = jnp.where(short_head == h, wides[job][h * ROWS:(h + 1) * ROWS], kept)
+            dq_ref[rows[each], cols[job]] = (kept * factor).astype(BF)
+            heads = slice(pack * PACK, (pack + 1) * PACK)
+            s_ref[images[each], heads, :] += weights[job] * scales[each]
+            dk_ref[images[each], :, cols[job]] += d_keys[job]
+        for each in reversed(range(together)):
+            total = jnp.zeros((1, padded), F32)
+            for job, (owner, pack) in enumerate(jobs):
+                if owner == each:
+                    total = total + jnp.sum(weights[job] * gains[job], axis=0, keepdims=True)
+            live = slots[each] < used
+            spot = pl.ds(jnp.where(live, wheres[each], outs), 1)
+            lg_ref[spot, :] = total * (1.0 / text_len)
         return carry
 
-    lax.fori_loop(0, used, pair, 0)
-
-    def one_hot(feat):
-        lanes = lax.broadcasted_iota(jnp.int32, (feat.shape[0], model), 1)
-        return jnp.where(lanes == feat, 1.0, 0.0).astype(BF)
+    lax.fori_loop(0, (used + together - 1) // together, pairs, 0)
 
     blocks, tall_rows, half = gq_ref.shape
     lines = tall_rows // 2
@@ -159,15 +190,12 @@
         ]
         out_ref[...] = jnp.concatenate(sides, axis=1).astype(BF)
 
-    turn_q = one_hot(feat_q_ref[...])
+    turn_q = one_hot(feat_q_ref[...], model)
     store(gq_ref, nt(turn_q, tp_ref[...]).astype(BF), dq_ref[...])
-    turn_k = one_hot(feat_k_ref[...])
-    pictures = x_ref[...].reshape(count * padded, model)
-    flipped = nt(turn_k, pictures).astype(BF)
+    flipped = flip_ref[...]
     store(gk_ref, flipped, (dk_ref[...] * factor).astype(BF).reshape(count * padded, model))
 
-    answers = jnp.sum(lg_ref[...], axis=1, keepdims=True)
-    outs = answers.shape[0]
+    answers = jnp.sum(lg_ref[:outs], axis=1, keepdims=True)
     lane = lax.broadcasted_iota(jnp.int32, (outs, 128), 1)
     line = lax.broadcasted_iota(jnp.int32, (outs, 128), 0)
     rest = jnp.where(lane - 16 == line % (3 * count), answers, 0.0)
@@ -326,7 +354,7 @@
     capacity = max(2, (2 * count + devices - 1) // devices)
     padded = up(length, 256)
     texts = devices * count
-    slots = count + devices * capacity
+    slots = up(count + devices * capacity, 2)
 
     owner = negatives // count
     meta = jnp.concatenate(
@@ -338,32 +366,33 @@
     )
     everyone = lax.all_gather(message, "dev", axis=0, tiled=True)
 
-    keys, gains, pictures = pl.pallas_call(
-        keys_kernel,
-        out_shape=(
-            jax.ShapeDtypeStruct((count, padded, model), BF),
-            jax.ShapeDtypeStruct((count, 16, padded), F32),
-            jax.ShapeDtypeStruct((count, padded, model), BF),
-        ),
-        in_specs=[VMEM] * 3,
-        out_specs=(VMEM,) * 3,
-        compiler_params=pltpu.CompilerParams(vmem_limit_bytes=BIG),
-        cost_estimate=pl.CostEstimate(
-            flops=4 * count * padded * model * model, bytes_accessed=8 * 1024 * 1024,
-            transcendentals=0,
-        ),
-    )(image_tokens, kv_weight, match_head.reshape(1, model))
-
-    facts = everyone[:, text_len, :8].astype(F32)
-    owners = facts[:, 3:5].astype(jnp.int32).reshape(-1)
-    locals_ = facts[:, 5:7].astype(jnp.int32).reshape(-1)
-    tangents = facts[:, :3].reshape(-1)
     total = groups * devices
     rows = model // total
     lines = up(rows, 8)
     half = model // 2
     orders = bit_orders(groups, devices)
     feat_k, feat_q = (feature_rows(model, total, order) for order in orders)
+    keys, gains, flipped = pl.pallas_call(
+        keys_kernel,
+        out_shape=(
+            jax.ShapeDtypeStruct((count, padded, model), BF),
+            jax.ShapeDtypeStruct((count, 16, padded), F32),
+            jax.ShapeDtypeStruct((total * lines, count * padded), BF),
+        ),
+        in_specs=[VMEM] * 4,
+        out_specs=(VMEM,) * 3,
+        scratch_shapes=[pltpu.VMEM((count, padded, model), BF)],
+        compiler_params=pltpu.CompilerParams(vmem_limit_bytes=BIG),
+        cost_estimate=pl.CostEstimate(
+            flops=4 * count * padded * model * model, bytes_accessed=8 * 1024 * 1024,
+            transcendentals=0,
+        ),
+    )(image_tokens, kv_weight, match_head.reshape(1, model), feat_k)
+
+    facts = everyone[:, text_len, :8].astype(F32)
+    owners = facts[:, 3:5].astype(jnp.int32).reshape(-1)
+    locals_ = facts[:, 5:7].astype(jnp.int32).reshape(-1)
+    tangents = facts[:, :3].reshape(-1)
     home = np.argsort(places(total, orders[0])).astype(np.int32) * lines
     home = np.repeat(home, count * 3).reshape(groups, 1, texts * 3)
     home = lax.dynamic_index_in_dim(jnp.asarray(home), lax.axis_index("grp"), 0, keepdims=False)
@@ -374,7 +403,7 @@
             jax.ShapeDtypeStruct((total, 2 * lines, half), BF),
             jax.ShapeDtypeStruct((total, lines, 128), F32),
         ),
-        in_specs=[SMEM] * 3 + [VMEM] * 8,
+        in_specs=[SMEM] * 3 + [VMEM] * 7,
         out_specs=(VMEM,) * 3,
         scratch_shapes=[
             pltpu.VMEM((slots * ROWS, model), BF),
@@ -382,7 +411,7 @@
             pltpu.VMEM((count, padded, model), F32),
             pltpu.VMEM((slots * ROWS, model), BF),
             pltpu.VMEM((count, 128, padded), F32),
-            pltpu.VMEM((texts * 3, padded), F32),
+            pltpu.VMEM((texts * 3 + 8, padded), F32),
             pltpu.SMEM((slots,), jnp.int32),
             pltpu.SMEM((slots,), jnp.int32),
             pltpu.SMEM((slots,), jnp.int32),
@@ -391,7 +420,7 @@
         cost_estimate=pl.CostEstimate(
             flops=20 * 1024**3, bytes_accessed=16 * 1024 * 1024, transcendentals=0
         ),
-    )(owners, locals_, tangents, feat_k, feat_q, home, pictures, keys, gains, everyone,
+    )(owners, locals_, tangents, feat_q, home, flipped, keys, gains, everyone,
       query_weight)
 
     steps = len(orders[0])

time: 128 us -> 105 us (0.82)
  Pallas kernels: 80.7 us -> 60.3 us
  waiting for transfers between devices: 15.4 us -> 13.6 us
    pallas_call x1, Pallas kernels: 44.2 us -> 30.1 us  [local(): pl.pallas_call(functools.partial(reduce_kernel, rows, orders), out_shape=...]
    pallas_call x1, Pallas kernels: 29 us -> 20.9 us  [local(): pl.pallas_call(functools.partial(pairs_kernel, length, text_len), out_sha...]
    pallas_call x1, Pallas kernels: 7.59 us -> 9.35 us  [local(): pl.pallas_call(keys_kernel, out_shape=(jax.ShapeDtypeStruct((count, padde...]
    all_gather x1, waiting for transfers between devices: 15.4 us -> 13.6 us  [local(): everyone = lax.all_gather(message, 'dev', axis=0, tiled=True)]
  transfers between devices with their start and end apart: 1 -> 1, of which waited for: 1 -> 1; matrix products, arithmetic and copies ran while one was open for 4% -> 5% of each run, Pallas kernels for 6% -> 9%
where the time goes in v3:
time: 105 us
  Pallas kernels  60.3 us (57%)
  local copies, waits for them, and re-layouts  14.2 us (14%)
  between operations  14.1 us (13%)
  waiting for transfers between devices  13.6 us (13%)
  other arithmetic  2.49 us (2%)
    pallas_call x1, Pallas kernels, local(): pl.pallas_call(functools.partial(reduce_kernel, rows, orders), out_shape=...  30.1 us
    pallas_call x1, Pallas kernels, local(): pl.pallas_call(functools.partial(pairs_kernel, length, text_len), out_sha...  20.9 us
    all_gather x1, waiting for transfers between devices, local(): everyone = lax.all_gather(message, 'dev', axis=0, tiled=True)  13.6 us
    pallas_call x1, Pallas kernels, local(): pl.pallas_call(keys_kernel, out_shape=(jax.ShapeDtypeStruct((count, padde...  9.35 us
    unnamed x13, local copies, waits for them, and re-layouts  9.03 us
  transfers between devices with their start and end apart: 1, of which 1 were waited for; matrix products, arithmetic and copies ran while one was open for 5% of the time, Pallas kernels for 9%

profile of v3, /device:TPU:0, one launch (start us, length us, event | category | flops | bytes accessed | tf_op | source)
XLA Modules:
  0.0 104.8 jit_solution(4821534604547640387)
XLA Ops:
  7.2 0.0 all-gather.2.cloned.1.call-start
  7.2 0.8 copy.28
  8.0 0.8 fusion.5
  8.8 0.9 copy.33
  9.7 0.1 pad.7.clone
  9.8 0.8 maximum_maximum_fusion
  10.6 0.0 all-gather.2.cloned.1.call-update
  10.6 1.3 %reshape.24.mh_ref = f32[1,768]{1,0:T(1,128)} reshape(f32[768]{0:T(1024)} %param.15) | data formatting | bytes 6144 | tf_op jit(solution)/shard_map/reshape | solution.py:390
  11.9 2.5 %copy.35.x_ref = bf16[4,197,768]{2,1,0:T(8,128)(2,1)} copy(bf16[4,197,768]{2,0,1:T(4,128)(2,1)} %param.10) | data formatting | bytes 2420736 | tf_op args[0]
  14.4 1.2 %dynamic-slice_bitcast_fusion.home_ref = s32[1,96]{1,0:T(1,128)} fusion(s32[4,1,96]{2,1,0:T(1,128)} %constant.38.clone, s32[]{:T(128)S(6)} %select_n.10), kind=kLoop, calls=%fused_computation.20 | loop fusion | bytes 772 | tf_op jit(solution)/shard_map/jit(dynamic_index_in_dim)/squeeze | solution.py:398
  15.6 9.4 %shard_map.121 = (bf16[4,256,768]{2,1,0:T(8,128)(2,1)}, f32[4,16,256]{2,1,0:T(8,128)}, bf16[768,1024]{1,0:T(8,128)(2,1)}) custom-call(bf16[4,197,768]{2,1,0:T(8,128)(2,1)} %copy.35.x_ref, bf16[768,1536]{1,0:T(8,128)(2,1)} %w_ref.1, f32[1,768]{1,0:T(1,128)} %reshape.24.mh_ref, s32[768,1]{1,0:T(8,128)} %constant.37.clone.feat_ref), custom_call_target="tpu_custom_call" | custom-call | flops 2415919104 | bytes 8388608 | tf_op jit(solution)/shard_map/pallas_call | solution.py:375
  24.9 13.6 %all-gather.2.cloned.1.call-done.t_ref = bf16[32,32,768]{2,1,0:T(8,128)(2,1)} async-done(((bf16[4,32,768]{2,1,0:T(8,128)(2,1)}), bf16[32,32,768]{2,1,0:T(8,128)(2,1)}) %all-gather.2.cloned.1.call-update) | async-done | bytes 1572880 | tf_op jit(solution)/shard_map/all_gather | solution.py:367
  38.5 0.9 slice_convert_fusion.2
  39.4 0.1 slice_convert_fusion
  39.5 0.7 reshape.23.tangent_ref
  40.1 0.6 reshape.22.local_ref
  40.8 0.6 reshape.21.owner_ref
  41.4 0.0 copy-start.3
  41.4 20.9 %shard_map.122 = (bf16[32,48,384]{2,1,0:T(8,128)(2,1)}, bf16[32,48,384]{2,1,0:T(8,128)(2,1)}, f32[32,24,128]{2,1,0:T(8,128)}) custom-call(s32[64]{0:T(128)} %reshape.21.owner_ref, s32[64]{0:T(128)} %reshape.22.local_ref, f32[96]{0:T(128)} %reshape.23.tangent_ref, s32[768,1]{1,0:T(8,128)} %constant.39.clone.feat_q_ref, ...), custom_call_target="tpu_custom_call" | custom-call | flops 21474836480 | bytes 16777216 | tf_op jit(solution)/shard_map/pallas_call | solution.py:399
  62.3 0.0 copy-done.3
  62.3 0.0 copy-start
  62.3 1.3 %copy-done = bf16[32,48,384]{2,1,0:T(8,128)(2,1)S(1)} copy-done((bf16[32,48,384]{2,1,0:T(8,128)(2,1)S(1)}, bf16[32,48,384]{2,1,0:T(8,128)(2,1)}, u32[]{:S(2)}) %copy-start) | copy-done | bytes 1179672
  63.5 0.0 copy-start.1
  63.5 1.3 %copy-done.1 = bf16[32,48,384]{2,1,0:T(8,128)(2,1)S(1)} copy-done((bf16[32,48,384]{2,1,0:T(8,128)(2,1)S(1)}, bf16[32,48,384]{2,1,0:T(8,128)(2,1)}, u32[]{:S(2)}) %copy-start.1) | copy-done | bytes 1179672
  64.8 0.0 copy-start.2
  64.8 1.0 copy-done.2
  65.8 30.1 %shard_map.123 = (f32[24,768]{1,0:T(8,128)S(1)}, f32[24,1536]{1,0:T(8,128)S(1)}, f32[8,128]{1,0:T(8,128)S(1)}) custom-call(bf16[32,48,384]{2,1,0:T(8,128)(2,1)S(1)} %copy-done, bf16[32,48,384]{2,1,0:T(8,128)(2,1)S(1)} %copy-done.1, f32[32,24,128]{2,1,0:T(8,128)S(1)} %copy-done.2, f32[1,768]{1,0:T(1,128)S(1)} %copy-done.3), custom_call_target="tpu_custom_call" | custom-call | flops 1048576 | bytes 8388608 | tf_op jit(solution)/shard_map/pallas_call | solution.py:427
  95.9 0.1 slice_reduce_fusion
  96.0 0.7 reshape_squeeze.3
  96.6 0.6 copy.38
  97.3 0.7 copy.39
  (2 shorter events, 0.0 us)
Async XLA Ops:
  7.2 31.4 %all-gather.2.cloned.1.call-start = ((), (), s32[]{:S(2)}) async-start(), calls=%async_computation | async-start | bytes 1769472 | tf_op jit(solution)/shard_map/all_gather | solution.py:367
  41.4 20.9 %copy-start.3 = (f32[1,768]{1,0:T(1,128)S(1)}, f32[1,768]{1,0:T(1,128)}, u32[]{:S(2)}) copy-start(f32[1,768]{1,0:T(1,128)} %reshape.24.mh_ref) | copy-start | bytes 9220
  62.3 1.3 %copy-start = (bf16[32,48,384]{2,1,0:T(8,128)(2,1)S(1)}, bf16[32,48,384]{2,1,0:T(8,128)(2,1)}, u32[]{:S(2)}) copy-start(bf16[32,48,384]{2,1,0:T(8,128)(2,1)} %get-tuple-element.15.k_ref) | copy-start | bytes 3538948
  63.5 1.3 %copy-start.1 = (bf16[32,48,384]{2,1,0:T(8,128)(2,1)S(1)}, bf16[32,48,384]{2,1,0:T(8,128)(2,1)}, u32[]{:S(2)}) copy-start(bf16[32,48,384]{2,1,0:T(8,128)(2,1)} %get-tuple-element.16.q_ref) | copy-start | bytes 3538948
  64.8 1.0 copy-start.2
Sparse Core Ops, SparseCore 0:
  10.7 27.7 all-gather.1
